TPU v7x, 32 devices: a whole 2x2x4 slice. The times are simulated.
32 devices in a mesh: groups: 2 (over y), length: 4 (over z), sector: 2 (over x), pair: 2 (over core).
Axes of the slice: x: 2, y: 2, z: 4, core: 2. Of those that a mesh axis runs over, the one named last changes fastest.
Arguments:
- flag_kernels: bfloat16 [4, 8, 32, 25, 1024], P('length', ('groups', 'sector', 'pair')), parts along dimension 1, may hold values from -1.1953125 to 1.1953125
- flag_unary: bfloat16 [4, 8, 32, 8, 1024], P('length', ('groups', 'sector', 'pair')), parts along dimension 1, may hold values from -8 to 8
- flag_labels: int32 [4, 8, 32, 1024], P('length', ('groups', 'sector', 'pair')), parts along dimension 1, may hold values from 0 to 7
- flag_mask: int32 [4, 8, 32, 1024], P('length', ('groups', 'sector', 'pair')), parts along dimension 1, may hold values 0 or 1
- dest_list: int32 [4, 8, 32], P('length', ('groups', 'sector', 'pair')), parts along dimension 1, may hold values from -1 to 3, as said below
- slot_list: int32 [4, 8, 32], P('length', ('groups', 'sector', 'pair')), parts along dimension 1, may hold values from -1 to 15, as said below
- res_kernels: bfloat16 [4, 8, 8, 25, 1024], P('length', ('groups', 'sector', 'pair')), parts along dimension 1, may hold values from -1.1953125 to 1.1953125
- res_unary: bfloat16 [4, 8, 8, 8, 1024], P('length', ('groups', 'sector', 'pair')), parts along dimension 1, may hold values from -8 to 8
- res_labels: int32 [4, 8, 8, 1024], P('length', ('groups', 'sector', 'pair')), parts along dimension 1, may hold values from 0 to 7
- res_mask: int32 [4, 8, 8, 1024], P('length', ('groups', 'sector', 'pair')), parts along dimension 1, may hold values 0 or 1
Outputs:
- flag_grad: bfloat16 [4, 8, 32, 25, 1024], P('length', ('groups', 'sector', 'pair')), parts along dimension 1
- res_grad: bfloat16 [4, 8, 8, 25, 1024], P('length', ('groups', 'sector', 'pair')), parts along dimension 1
- helper_loss: float32 [4, 8, 16], P('length', ('groups', 'sector', 'pair')), parts along dimension 1
There are 2 independent parts, one for each index of `groups`. A program takes and returns all parts, laid end to end along the dimension named above; each array names one. Nothing has to cross between parts.
Inputs may be any that keep to these rules, and one draw needn't show every extreme that they name: `dest_list`: entry j of a device's list is -1 exactly when its slot j holds no flagged tile, and the -1 entries come after all others; at most 8 entries of one device name the same destination. `slot_list`: for each index along sector and pair, each pair of a destination along length and a slot 0 to 15 is named by exactly one entry of the lists of the devices along length; an entry is -1 exactly where dest_list is -1.
All inputs are finite; a program needn't handle non-finite values. No bound on the sum of `flag_mask` or of `res_mask` on one device may be relied on, other than what follows from the above.
Results may differ from a plain program's by a relative error of at most 0.001.
Values may be sent and summed in bfloat16 or wider, within the bound.
A program may use at most 64 MiB of HBM per device.

v0:
```python
import functools

import jax
import jax.numpy as jnp
from jax import lax
from jax.experimental import pallas as pl
from jax.experimental.pallas import tpu as pltpu
from jax.sharding import PartitionSpec as P

CLASSES = 8
TAPS = 25
TILE = 32
ITERS = 3
RECV = 16
BATCH = 16
TOGETHER = 2

OFFSETS = [(a, b) for a in range(-2, 3) for b in range(-2, 3)]


def shift_all(x, lane):
    after = pltpu.roll(x, 7, 0)
    before = pltpu.roll(x, 1, 0)
    shifted = []
    for a, b in OFFSETS:
        k = a * TILE + b
        if k == 0:
            shifted.append(x)
        elif k > 0:
            shifted.append(pltpu.roll(jnp.where(lane >= k, x, after), 128 - k, 1))
        else:
            shifted.append(pltpu.roll(jnp.where(lane < 128 + k, x, before), -k, 1))
    return shifted


def shift_one(x, k, lane):
    if k == 0:
        return x
    if k > 0:
        return pltpu.roll(jnp.where(lane >= k, x, pltpu.roll(x, 7, 0)), 128 - k, 1)
    return pltpu.roll(jnp.where(lane < 128 + k, x, pltpu.roll(x, 1, 0)), -k, 1)


def total(values):
    while len(values) > 1:
        values = [sum(values[i : i + 2]) for i in range(0, len(values), 2)]
    return values[0]


def tile(j, tgt_ref, loss_ref, flat, unary, kfwd, kbwd, shf):
    lane = lax.broadcasted_iota(jnp.int32, (8, 128), 1)
    sub = lax.broadcasted_iota(jnp.int32, (8, 128), 0)
    row = sub * 4 + lane // TILE
    col = lane % TILE

    def inside(t):
        a, b = OFFSETS[t]
        return (row + a >= 0) & (row + a < TILE) & (col + b >= 0) & (col + b < TILE)

    for t in range(TAPS):
        a, b = OFFSETS[t]
        masked = jnp.where(inside(t), flat[pl.ds(pl.multiple_of(j * (TAPS * 8) + 8 * t, 8), 8), :], 0.0)
        kfwd[t] = masked
        kbwd[TAPS - 1 - t] = shift_one(masked, -(a * TILE + b), lane)

    yield

    def send(field, weights, keep):
        result = []
        for c in range(CLASSES):
            moved = shift_all(field[c], lane)
            if keep is not None:
                for t in range(TAPS):
                    shf[keep, t, c] = moved[t]
            sums = [moved[t] * weights[t] for t in range(5)]
            for t in range(5, TAPS):
                sums[t % 5] = sums[t % 5] + moved[t] * weights[t]
            result.append(total(sums))
        return result

    def soft(logits):
        raised = [jnp.exp(x) for x in logits]
        summed = total(raised)
        scale = 1.0 / summed
        return [x * scale for x in raised], summed

    first = [unary[pl.ds(pl.multiple_of(j * (CLASSES * 8) + 8 * c, 8), 8), :] for c in range(CLASSES)]
    beliefs, _ = soft(first)
    kept = [beliefs]
    for i in range(ITERS):
        sent = send(beliefs, kfwd, i)
        yield
        logits = [unary[pl.ds(pl.multiple_of(j * (CLASSES * 8) + 8 * c, 8), 8), :] + sent[c] for c in range(CLASSES)]
        beliefs, summed = soft(logits)
        yield
        kept.append(beliefs)
    labels = tgt_ref[j]
    used = labels < CLASSES
    chosen = total([jnp.where(labels == c, logits[c], 0.0) for c in range(CLASSES)])
    loss_ref[j] = jnp.where(used, jnp.log(summed) - chosen, 0.0)
    slope = [
        jnp.where(used, kept[3][c] - jnp.where(labels == c, 1.0, 0.0), 0.0)
        for c in range(CLASSES)
    ]
    slopes = [None, None, slope]
    for i in (1, 0):
        back = send(slopes[i + 1], kbwd, None)
        yield
        field = kept[i + 1]
        mean = total([field[c] * back[c] for c in range(CLASSES)])
        slopes[i] = [field[c] * (back[c] - mean) for c in range(CLASSES)]
        yield
    for t in range(TAPS):
        chains = [slopes[0][c] * shf[0, t, c] for c in range(4)]
        for n in range(4, ITERS * CLASSES):
            i, c = n // CLASSES, n % CLASSES
            chains[n % 4] = chains[n % 4] + slopes[i][c] * shf[i, t, c]
        gathered = total(chains)
        flat[pl.ds(pl.multiple_of(j * (TAPS * 8) + 8 * t, 8), 8), :] = jnp.where(inside(t), gathered, 0.0)


def crf_kernel(dest_ref, k_ref, u_ref, tgt_ref, grad_ref, loss_ref, *scratch):
    step = tgt_ref.shape[0]
    base = pl.program_id(0) * step
    flat, unary = scratch[:2]
    for p in range(8):
        part = slice(128 * p, 128 * (p + 1))
        for t in range(TAPS):
            flat[pl.ds(8 * t + p, step, stride=8 * TAPS), :] = k_ref[0, 0, t, :, part].astype(
                jnp.float32
            )

    def clear(j):
        start = pl.multiple_of(j * (TAPS * 8), 8)
        flat[pl.ds(start, TAPS * 8), :] = jnp.zeros((TAPS * 8, 128), jnp.float32)
        loss_ref[j] = jnp.zeros((8, 128), jnp.float32)

    @pl.loop(0, step // TOGETHER)
    def _(n):
        members = [n * TOGETHER + w for w in range(TOGETHER)]
        listed = [dest_ref[base + j] >= 0 for j in members]

        @pl.when(functools.reduce(jnp.logical_or, listed))
        def _():
            for j in members:
                for p in range(8):
                    part = slice(128 * p, 128 * (p + 1))
                    start = j * (CLASSES * 8) + p
                    unary[pl.ds(start, CLASSES, stride=8), :] = u_ref[0, 0, j, :, part].astype(
                        jnp.float32
                    )
            steps = [
                tile(j, tgt_ref, loss_ref, flat, unary, *[ref.at[w] for ref in scratch[2:]])
                for w, j in enumerate(members)
            ]
            for _ in zip(*steps):
                pass
            for rest in steps[1:]:
                for _ in rest:
                    pass

        for j, known in zip(members, listed):
            pl.when(jnp.logical_not(known))(functools.partial(clear, j))

    for p in range(8):
        part = slice(128 * p, 128 * (p + 1))
        for t in range(TAPS):
            grad_ref[0, 0, t, :, part] = flat[
                pl.ds(8 * t + p, step, stride=8 * TAPS), :
            ].astype(jnp.bfloat16)


def crf(listed, kernels, unary, labels, mask):
    amount, taps, pixels = kernels.shape[2:]
    step = min(BATCH, amount)
    kernels = jnp.swapaxes(kernels, 2, 3)
    taps_first = pl.BlockSpec((1, 1, taps, step, pixels), lambda i, s: (0, 0, 0, i, 0))
    scores = pl.BlockSpec((1, 1, step, CLASSES, pixels), lambda i, s: (0, 0, i, 0, 0))
    fields = pl.BlockSpec((step, 8, 128), lambda i, s: (i, 0, 0))
    target = jnp.where(mask == 1, labels, CLASSES).reshape(amount, 8, 128)
    grad, loss = pl.pallas_call(
        crf_kernel,
        grid_spec=pltpu.PrefetchScalarGridSpec(
            num_scalar_prefetch=1,
            grid=(amount // step,),
            in_specs=[taps_first, scores, fields],
            out_specs=[taps_first, fields],
            scratch_shapes=[
                pltpu.VMEM((step * TAPS * 8, 128), jnp.float32),
                pltpu.VMEM((step * CLASSES * 8, 128), jnp.float32),
                pltpu.VMEM((TOGETHER, TAPS, 8, 128), jnp.float32),
                pltpu.VMEM((TOGETHER, TAPS, 8, 128), jnp.float32),
                pltpu.VMEM((TOGETHER, ITERS, TAPS, CLASSES, 8, 128), jnp.float32),
            ],
        ),
        out_shape=[
            jax.ShapeDtypeStruct(kernels.shape, jnp.bfloat16),
            jax.ShapeDtypeStruct((amount, 8, 128), jnp.float32),
        ],
        compiler_params=pltpu.CompilerParams(vmem_limit_bytes=32 * 1024 * 1024),
    )(listed, kernels, unary, target)
    return jnp.swapaxes(grad, 2, 3), loss


def on_device(fk, fu, fl, fm, dest, slot, rk, ru, rl, rm):
    destinations, slots = dest[0, 0], slot[0, 0]
    flag_grad, partial = crf(destinations, fk, fu, fl, fm)
    count = lax.axis_size("length")
    losses = jnp.sum(partial, axis=(1, 2)) / TILE
    place = jnp.where(destinations >= 0, destinations * RECV + slots, -1)
    table = jnp.sum(
        jnp.where(place[None, :] == jnp.arange(count * RECV)[:, None], losses[None, :], 0.0), axis=1
    )
    got = lax.all_to_all(
        table.reshape(count, RECV), "length", split_axis=0, concat_axis=0, tiled=True
    )
    res_grad, _ = crf(jnp.zeros((rk.shape[2],), jnp.int32), rk, ru, rl, rm)
    return flag_grad, res_grad, jnp.sum(got, axis=0)[None, None]


def solution(mesh):
    tile_axes = ("groups", "sector", "pair")
    spec = lambda n: P("length", tile_axes, *([None] * n))
    return jax.shard_map(
        on_device,
        mesh=mesh,
        in_specs=(spec(3), spec(3), spec(2), spec(2), spec(1), spec(1), spec(3), spec(3), spec(2), spec(2)),
        out_specs=(spec(3), spec(3), spec(1)),
        check_vma=False,
    )
```

profile of v0, /device:TPU:0, one launch (start us, length us, event | category | flops | bytes accessed | tf_op | source)
XLA Modules:
  0.0 66.9 jit_solution(17621657274615283050)
XLA Ops:
  0.6 0.0 copy-start.5
  0.6 0.0 copy-start.8
  0.7 0.0 copy-start.6
  0.7 0.0 copy-start.7
  0.7 0.0 copy-start.2
  0.7 0.0 copy-start.3
  0.7 1.0 %select_bitcast_fusion = s32[4,8,8,128]{3,1,2,0:T(8,128)S(1)} fusion(s32[1,1,32,1024]{3,2,1,0:T(8,128)} %param.12, s32[1,1,32,1024]{3,2,1,0:T(8,128)} %param.13), kind=kLoop, calls=%fused_computation | loop fusion | flops 65536 | bytes 393216
  1.8 0.0 copy-start
  1.8 1.4 %copy-done = bf16[1,1,32,25,1024]{4,2,3,1,0:T(8,128)(2,1)S(1)} copy-done((bf16[1,1,32,25,1024]{4,2,3,1,0:T(8,128)(2,1)S(1)}, bf16[1,1,32,25,1024]{4,2,3,1,0:T(8,128)(2,1)}, u32[]{:S(2)}) %copy-start) | copy-done | bytes 1638424
  3.2 0.0 copy-start.1
  3.2 1.0 %copy-done.1 = bf16[1,1,32,8,1024]{4,3,2,1,0:T(8,128)(2,1)S(1)} copy-done((bf16[1,1,32,8,1024]{4,3,2,1,0:T(8,128)(2,1)S(1)}, bf16[1,1,32,8,1024]{4,3,2,1,0:T(8,128)(2,1)}, u32[]{:S(2)}) %copy-start.1) | copy-done | bytes 524312
  4.3 0.0 copy-start.4
  4.3 0.7 copy-done.4
  4.9 3.8 %shard_map.121 = (bf16[1,1,25,32,1024]{4,3,2,1,0:T(8,128)(2,1)}, f32[32,8,128]{2,1,0:T(8,128)S(1)}) custom-call(s32[32]{0:T(128)S(1)} %bitcast.28, bf16[1,1,25,32,1024]{4,3,2,1,0:T(8,128)(2,1)S(1)} %bitcast.24, bf16[1,1,32,8,1024]{4,3,2,1,0:T(8,128)(2,1)S(1)} %copy-done.1, s32[32,8,128]{2,1,0:T(8,128)S(1)} %bitcast.25), custom_call_target="tpu_custom_call" | custom-call | tf_op jit(solution)/shard_map/pallas_call | solution.py:181
  8.7 0.3 reduce_sum.27
  9.0 0.0 copy-done.5
  9.0 0.0 copy-done.8
  9.0 0.1 select_reduce_fusion
  9.1 0.7 %all_to_all.6 = f32[4,1,16]{2,0,1:T(4,128)} reshape(f32[64]{0:T(128)S(1)} %select_reduce_fusion) | data formatting | bytes 512 | tf_op jit(solution)/shard_map/all_to_all | solution.py:214
  9.8 44.6 %all-to-all-start = ((f32[4,1,16]{2,1,0:T(1,128)}), f32[4,1,16]{2,1,0:T(1,128)S(1)}, u32[]{:S(2)}, u32[]{:S(2)}) async-start(f32[4,1,16]{2,1,0:T(1,128)} %bitcast.6), calls=%async_computation | async-start | bytes 4096 | tf_op jit(solution)/shard_map/all_to_all | solution.py:214
  54.4 0.0 copy-done.6
  54.4 0.0 copy-done.7
  54.5 0.0 copy-done.2
  54.5 0.0 copy-done.3
  54.5 11.9 %shard_map.122 = (bf16[1,1,25,8,1024]{4,3,2,1,0:T(8,128)(2,1)}, f32[8,8,128]{2,1,0:T(8,128)}) custom-call(s32[8]{0:T(128)S(1)} %broadcast_1_dest_ref.2.dest_ref, bf16[1,1,25,8,1024]{4,3,2,1,0:T(8,128)(2,1)S(1)} %bitcast.26, bf16[1,1,8,8,1024]{4,3,2,1,0:T(8,128)(2,1)S(1)} %copy-done.3, s32[8,8,128]{2,1,0:T(8,128)S(1)} %bitcast.27), custom_call_target="tpu_custom_call" | custom-call | tf_op jit(solution)/shard_map/pallas_call | solution.py:181
  66.4 0.0 all-to-all-done
  66.4 0.5 reduce_sum.29
  (6 shorter events, 0.1 us)
Async XLA Ops:
  0.6 8.4 %copy-start.5 = (s32[1,1,32]{2,1,0:T(1,128)S(1)}, s32[1,1,32]{2,1,0:T(1,128)}, u32[]{:S(2)}) copy-start(s32[1,1,32]{2,1,0:T(1,128)} %param.14) | copy-start | bytes 388
  0.6 8.4 %copy-start.8 = (s32[1,1,32]{2,1,0:T(1,128)S(1)}, s32[1,1,32]{2,1,0:T(1,128)}, u32[]{:S(2)}) copy-start(s32[1,1,32]{2,1,0:T(1,128)} %param.15) | copy-start | bytes 388
  0.7 53.8 %copy-start.6 = (s32[1,1,8,1024]{3,2,1,0:T(8,128)S(1)}, s32[1,1,8,1024]{3,2,1,0:T(8,128)}, u32[]{:S(2)}) copy-start(s32[1,1,8,1024]{3,2,1,0:T(8,128)} %param.18) | copy-start | bytes 98308
  0.7 53.8 %copy-start.7 = (s32[1,1,8,1024]{3,2,1,0:T(8,128)S(1)}, s32[1,1,8,1024]{3,2,1,0:T(8,128)}, u32[]{:S(2)}) copy-start(s32[1,1,8,1024]{3,2,1,0:T(8,128)} %param.19) | copy-start | bytes 98308
  0.7 53.8 %copy-start.2 = (bf16[1,1,8,25,1024]{4,2,3,1,0:T(8,128)(2,1)S(1)}, bf16[1,1,8,25,1024]{4,2,3,1,0:T(8,128)(2,1)}, u32[]{:S(2)}) copy-start(bf16[1,1,8,25,1024]{4,2,3,1,0:T(8,128)(2,1)} %param.16) | copy-start | bytes 1228804
  0.7 53.8 %copy-start.3 = (bf16[1,1,8,8,1024]{4,3,2,1,0:T(8,128)(2,1)S(1)}, bf16[1,1,8,8,1024]{4,3,2,1,0:T(8,128)(2,1)}, u32[]{:S(2)}) copy-start(bf16[1,1,8,8,1024]{4,3,2,1,0:T(8,128)(2,1)} %u_ref.3) | copy-start | bytes 393220
  1.8 1.4 %copy-start = (bf16[1,1,32,25,1024]{4,2,3,1,0:T(8,128)(2,1)S(1)}, bf16[1,1,32,25,1024]{4,2,3,1,0:T(8,128)(2,1)}, u32[]{:S(2)}) copy-start(bf16[1,1,32,25,1024]{4,2,3,1,0:T(8,128)(2,1)} %param.10) | copy-start | bytes 4915204
  3.2 1.0 %copy-start.1 = (bf16[1,1,32,8,1024]{4,3,2,1,0:T(8,128)(2,1)S(1)}, bf16[1,1,32,8,1024]{4,3,2,1,0:T(8,128)(2,1)}, u32[]{:S(2)}) copy-start(bf16[1,1,32,8,1024]{4,3,2,1,0:T(8,128)(2,1)} %u_ref.2) | copy-start | bytes 1572868
  4.3 0.7 copy-start.4
  9.8 56.6 %all-to-all-start = ((f32[4,1,16]{2,1,0:T(1,128)}), f32[4,1,16]{2,1,0:T(1,128)S(1)}, u32[]{:S(2)}, u32[]{:S(2)}) async-start(f32[4,1,16]{2,1,0:T(1,128)} %bitcast.6), calls=%async_computation | async-start | bytes 4096 | tf_op jit(solution)/shard_map/all_to_all | solution.py:214
where the time goes:
time: 68.2 us; the launch traced here: 66.9 us
  starting transfers between devices  44.6 us (65%)
  Pallas kernels  15.6 us (23%)
  local copies, waits for them, and re-layouts  3.87 us (6%)
  other arithmetic  2 us (3%)
  between operations  0.75 us (1%)
    all_to_all x1, starting transfers between devices, on_device(): lax.all_to_all(table.reshape(count, RECV), 'length', split_axis=0, concat...  44.6 us
    pallas_call x2, Pallas kernels, crf(): pl.pallas_call(crf_kernel, grid_spec=pltpu.PrefetchScalarGridSpec(num_sca...  15.6 us
    unnamed x20, local copies, waits for them, and re-layouts  3.18 us
  transfers between devices with their start and end apart: 1, of which 0 were waited for; matrix products, arithmetic and copies ran while one was open for 0% of the time, Pallas kernels for 18%

commit v1 on v0

v1 whole, which is shorter than its diff:
```python
import jax
import jax.numpy as jnp
from jax import lax
from jax.experimental import pallas as pl
from jax.experimental.pallas import tpu as pltpu
from jax.sharding import PartitionSpec as P

CLASSES = 8
FREE = CLASSES - 1
TAPS = 25
TILE = 32
ITERS = 3
RECV = 16
LANES = 128
COLS = 4
PAIR = 2


def total(values):
    while len(values) > 1:
        values = [sum(values[i : i + 2]) for i in range(0, len(values), 2)]
    return values[0]


def nt(x, y):
    return lax.dot_general(x, y, (((1,), (1,)), ((), ())), preferred_element_type=jnp.float32)


def turned(x, carry):
    return x if carry == 0 else pltpu.roll(x, 7 if carry > 0 else 1, 0)


def passed(x, carry, tiles):
    return x if carry == 0 else pltpu.roll(x, LANES - tiles if carry > 0 else tiles, 1)


def message(kern, field, q):
    acc = [[None] * COLS for _ in range(FREE)]
    for a in range(5):
        for p in range(COLS + 4):
            near = [field[c, q + a, p] for c in range(FREE)]
            for o in range(COLS):
                b = p - o
                if 0 <= b < 5:
                    k = kern[5 * a + b, q, o]
                    for c in range(FREE):
                        x = k * near[c]
                        acc[c][o] = x if acc[c][o] is None else acc[c][o] + x
    return acc


def put_row(field, c, row, values):
    for p in range(-2, COLS + 2):
        field[c, row, p + 2] = turned(values[p % COLS], p // COLS)


def put_edges(field, rows, tiles):
    for c in range(FREE):
        for e in range(2):
            for source, target, carry in ((e, rows + e, 1), (rows - 2 + e, e - 2, -1)):
                values = [passed(field[c, source + 2, p + 2], carry, tiles) for p in range(COLS)]
                put_row(field, c, target + 2, values)


def crf_kernel(dest_ref, k_ref, u_ref, lab_ref, mask_ref, grad_ref, loss_ref, *scratch):
    kf, kb, raw, un, tgt, prob, fld, gfld, out = scratch
    tiles = lab_ref.shape[0]
    groups = LANES // tiles
    rows = TILE // groups
    depth = rows * TILE
    lane = lax.broadcasted_iota(jnp.int32, (8, LANES), 1)
    sub = lax.broadcasted_iota(jnp.int32, (8, LANES), 0)
    one = jnp.ones((8, LANES), jnp.float32)
    width = max(depth, LANES)
    halves = width // depth
    chunks = groups // halves
    low = lane // tiles % 2 == 0

    def spot(x):
        return x // TILE * TILE + x % 8 * COLS + x // 8 % COLS

    row = lax.broadcasted_iota(jnp.int32, (width, width), 0)
    col = lax.broadcasted_iota(jnp.int32, (width, width), 1)
    gather = jnp.where(col == row // depth * depth + spot(row % depth), 1.0, 0.0)
    gather = gather.astype(jnp.bfloat16)
    row = lax.broadcasted_iota(jnp.int32, (chunks * tiles, LANES), 0)
    col = lax.broadcasted_iota(jnp.int32, (chunks * tiles, LANES), 1)
    scatter = (row % tiles == col % tiles) & (row // tiles == col // (tiles * halves))
    scatter = jnp.where(scatter, 1.0, 0.0).astype(jnp.bfloat16)

    def to_fields(part):
        pieces = [part(g) for g in range(chunks) for _ in range(halves)]
        turn = nt(gather, jnp.concatenate(pieces, axis=0).astype(jnp.bfloat16))
        both = lambda n: turn[8 * n : 8 * n + 8]
        regs = [
            both(n) if halves == 1 else jnp.where(low, both(n), both(n + rows * COLS))
            for n in range(rows * COLS)
        ]
        return [regs[q * COLS : (q + 1) * COLS] for q in range(rows)]

    def inside(a, b, q, o):
        ok = None
        if not 0 <= o + b < COLS:
            ok = sub > 0 if o + b < 0 else sub < 7
        if not 0 <= q + a < rows:
            near = lane >= tiles if q + a < 0 else lane < LANES - tiles
            ok = near if ok is None else ok & near
        return ok

    for a in range(-2, 3):
        for b in range(-2, 3):
            t = 5 * (a + 2) + b + 2
            regs = to_fields(
                lambda g: k_ref[0, 0, t, :, width * g : width * (g + 1)].astype(jnp.float32)
            )
            for q in range(rows):
                for o in range(COLS):
                    ok = inside(a, b, q, o)
                    if ok is not None:
                        regs[q][o] = jnp.where(ok, regs[q][o], 0.0)
                    kf[t, q, o] = regs[q][o]
            for q in range(rows):
                for o in range(COLS):
                    x = turned(regs[(q - a) % rows][(o - b) % COLS], (o - b) // COLS)
                    kb[TAPS - 1 - t, q, o] = passed(x, (q - a) // rows, tiles)

    @pl.loop(0, tiles)
    def _(j):
        for p in range(8):
            raw[p, pl.ds(pl.multiple_of(j * CLASSES, CLASSES), CLASSES), :] = u_ref[
                0, 0, j, :, LANES * p : LANES * (p + 1)
            ].astype(jnp.float32)

    def scores(c):
        def part(g):
            span = width // LANES
            rows_of = pl.ds(c, tiles, stride=CLASSES)
            return jnp.concatenate([raw[span * g + n, rows_of, :] for n in range(span)], axis=1)

        return to_fields(part)

    last = scores(FREE)
    for c in range(FREE):
        own = scores(c)
        for q in range(rows):
            for o in range(COLS):
                un[c, q, o] = own[q][o] - last[q][o]

    listed = []
    for n in range(tiles // 8):
        x = jnp.zeros((8, LANES), jnp.int32)
        for j in range(8):
            x = jnp.where(sub == j, dest_ref[8 * n + j], x)
        listed.append(x)
    listed = jnp.concatenate(listed, axis=0)
    listed = jnp.concatenate([listed] * (width // LANES), axis=1)

    def targets(g):
        part = slice(width * g, width * (g + 1))
        used = (mask_ref[:, part] == 1) & (listed >= 0)
        return jnp.where(used, lab_ref[:, part], CLASSES).astype(jnp.float32)

    for q, regs in enumerate(to_fields(targets)):
        for o in range(COLS):
            tgt[q, o] = regs[o]

    def soft(i, q, logits):
        values = [[None] * COLS for _ in range(FREE)]
        for o in range(COLS):
            raised = [jnp.exp(logits[c][o]) for c in range(FREE)]
            scale = 1.0 / total(raised + [one])
            for c in range(FREE):
                belief = raised[c] * scale
                prob[i, c, q, o] = belief
                values[c][o] = belief - scale
        for c in range(FREE):
            put_row(fld.at[i], c, q + 2, values[c])

    @pl.loop(0, rows)
    def _(q):
        soft(0, q, [[un[c, q, o] for o in range(COLS)] for c in range(FREE)])

    put_edges(fld.at[0], rows, tiles)

    def sweep(i, q):
        sent = message(kf, fld.at[i], q)
        return [[un[c, q, o] + sent[c][o] for o in range(COLS)] for c in range(FREE)]

    @pl.loop(0, ITERS - 1)
    def _(i):
        @pl.loop(0, rows // PAIR)
        def _(m):
            for n in range(PAIR):
                q = PAIR * m + n
                soft(i + 1, q, sweep(i, q))

        put_edges(fld.at[i + 1], rows, tiles)

    def final(m, partial):
        for n in range(PAIR):
            q = PAIR * m + n
            logits = sweep(ITERS - 1, q)
            values = [[None] * COLS for _ in range(FREE)]
            for o in range(COLS):
                raised = [jnp.exp(logits[c][o]) for c in range(FREE)]
                summed = total(raised + [one])
                labels = tgt[q, o]
                used = labels < CLASSES
                picked = [labels == c for c in range(FREE)]
                chosen = total([jnp.where(picked[c], logits[c][o], 0.0) for c in range(FREE)])
                partial = partial + jnp.where(used, jnp.log(summed) - chosen, 0.0)
                scale = jnp.where(used, 1.0 / summed, 0.0)
                for c in range(FREE):
                    values[c][o] = raised[c] * scale - jnp.where(picked[c], 1.0, 0.0)
            for c in range(FREE):
                put_row(gfld.at[ITERS - 1], c, q + 2, values[c])
        return partial

    loss_ref[...] = lax.fori_loop(
        0, rows // PAIR, final, jnp.zeros((8, LANES), jnp.float32)
    )
    put_edges(gfld.at[ITERS - 1], rows, tiles)

    @pl.loop(0, ITERS - 1)
    def _(n):
        i = ITERS - 1 - n

        @pl.loop(0, rows // PAIR)
        def _(m):
            for n in range(PAIR):
                q = PAIR * m + n
                back = message(kb, gfld.at[i], q)
                values = [[None] * COLS for _ in range(FREE)]
                for o in range(COLS):
                    mean = total(
                        [back[c][o] * fld[i, c, q + 2, o + 2] for c in range(FREE)]
                    )
                    for c in range(FREE):
                        values[c][o] = prob[i, c, q, o] * (back[c][o] - mean)
                for c in range(FREE):
                    put_row(gfld.at[i - 1], c, q + 2, values[c])

        @pl.when(i > 1)
        def _():
            put_edges(gfld.at[i - 1], rows, tiles)

    @pl.loop(0, rows * 5)
    def _(n):
        q, a = n // 5, n % 5
        acc = [[None] * COLS for _ in range(5)]
        for i in range(ITERS):
            for c in range(FREE):
                slope = [gfld[i, c, q + 2, o + 2] for o in range(COLS)]
                for p in range(COLS + 4):
                    x = fld[i, c, q + a, p]
                    for o in range(COLS):
                        b = p - o
                        if 0 <= b < 5:
                            y = slope[o] * x
                            acc[b][o] = y if acc[b][o] is None else acc[b][o] + y
        place = lane // tiles * rows + q + a - 2
        ok = (place >= 0) & (place < TILE)
        for b in range(5):
            for o in range(COLS):
                near = ok
                if not 0 <= o + b - 2 < COLS:
                    near = near & (sub > 0 if o + b < 2 else sub < 7)
                spots = pl.ds(q * TILE + o, 8, stride=COLS)
                out[5 * a + b, spots, :] = jnp.where(near, acc[b][o], 0.0)

    for t in range(TAPS):
        flat = out[t]
        if halves > 1:
            low = lax.broadcasted_iota(jnp.int32, flat.shape, 1) // tiles % 2 == 0
            flat = jnp.concatenate([jnp.where(low, flat, 0.0), jnp.where(low, 0.0, flat)], axis=0)
        back = nt(scatter, flat.astype(jnp.bfloat16)).astype(jnp.bfloat16)
        for g in range(chunks):
            grad_ref[0, 0, t, :, width * g : width * (g + 1)] = back[tiles * g : tiles * (g + 1)]


def crf(listed, kernels, unary, labels, mask):
    amount, taps, pixels = kernels.shape[2:]
    rows = TILE * amount // LANES
    kernels = jnp.swapaxes(kernels, 2, 3)
    vmem = pl.BlockSpec(memory_space=pltpu.VMEM)
    regs = lambda *lead: pltpu.VMEM((*lead, 8, LANES), jnp.float32)
    grad, loss = pl.pallas_call(
        crf_kernel,
        in_specs=[pl.BlockSpec(memory_space=pltpu.SMEM), vmem, vmem, vmem, vmem],
        out_specs=[vmem, vmem],
        scratch_shapes=[
            regs(taps, rows, COLS),
            regs(taps, rows, COLS),
            pltpu.VMEM((8, amount * CLASSES, LANES), jnp.float32),
            regs(FREE, rows, COLS),
            regs(rows, COLS),
            regs(ITERS, FREE, rows, COLS),
            regs(ITERS, FREE, rows + 4, COLS + 4),
            regs(ITERS, FREE, rows + 4, COLS + 4),
            pltpu.VMEM((taps, rows * TILE, LANES), jnp.float32),
        ],
        out_shape=[
            jax.ShapeDtypeStruct(kernels.shape, jnp.bfloat16),
            jax.ShapeDtypeStruct((8, LANES), jnp.float32),
        ],
        compiler_params=pltpu.CompilerParams(vmem_limit_bytes=44 * 1024 * 1024),
    )(listed, kernels, unary, labels[0, 0], mask[0, 0])
    return jnp.swapaxes(grad, 2, 3), loss.reshape(8, LANES // amount, amount)


def on_device(fk, fu, fl, fm, dest, slot, rk, ru, rl, rm):
    destinations, slots = dest[0, 0], slot[0, 0]
    flag_grad, partial = crf(destinations, fk, fu, fl, fm)
    count = lax.axis_size("length")
    losses = jnp.sum(partial, axis=(0, 1)) / TILE
    place = jnp.where(destinations >= 0, destinations * RECV + slots, -1)
    table = jnp.sum(
        jnp.where(place[None, :] == jnp.arange(count * RECV)[:, None], losses[None, :], 0.0), axis=1
    )
    got = lax.all_to_all(
        table.reshape(count, RECV), "length", split_axis=0, concat_axis=0, tiled=True
    )
    res_grad, _ = crf(jnp.zeros((rk.shape[2],), jnp.int32), rk, ru, rl, rm)
    return flag_grad, res_grad, jnp.sum(got, axis=0)[None, None]


def solution(mesh):
    tile_axes = ("groups", "sector", "pair")
    spec = lambda n: P("length", tile_axes, *([None] * n))
    return jax.shard_map(
        on_device,
        mesh=mesh,
        in_specs=(spec(3), spec(3), spec(2), spec(2), spec(1), spec(1), spec(3), spec(3), spec(2), spec(2)),
        out_specs=(spec(3), spec(3), spec(1)),
        check_vma=False,
    )
```

time: 68.2 us -> 42.1 us (0.62); the launches traced: 66.9 us -> 41.8 us
  starting transfers between devices: 44.6 us -> 6.33 us
  Pallas kernels: 15.6 us -> 28.4 us
  local copies, waits for them, and re-layouts: 3.87 us -> 5.71 us
  other arithmetic: 2 us -> 0.68 us
    all_to_all x1, starting transfers between devices: 44.6 us -> 6.33 us  [on_device(): lax.all_to_all(table.reshape(count, RECV), 'length', split_axis=0, concat...]
    pallas_call x2, Pallas kernels: 15.6 us -> 28.4 us  [crf(): pl.pallas_call(crf_kernel, in_specs=[pl.BlockSpec(memory_space=pltpu.SMEM...]
    unnamed x20 -> x22, local copies, waits for them, and re-layouts: 3.18 us -> 4.96 us
    unnamed x2 -> x0, other arithmetic: 1.05 us -> none
  transfers between devices with their start and end apart: 1 -> 1, of which waited for: 0 -> 0; matrix products, arithmetic and copies ran while one was open for 0% -> 0% of each run, Pallas kernels for 18% -> 19%
where the time goes in v1:
time: 42.1 us; the launch traced here: 41.8 us
  Pallas kernels  28.4 us (67%)
  starting transfers between devices  6.33 us (15%)
  local copies, waits for them, and re-layouts  5.71 us (14%)
  between operations  0.71 us (2%)
  other arithmetic  0.68 us (2%)
    pallas_call x2, Pallas kernels, crf(): pl.pallas_call(crf_kernel, in_specs=[pl.BlockSpec(memory_space=pltpu.SMEM...  28.4 us
    all_to_all x1, starting transfers between devices, on_device(): lax.all_to_all(table.reshape(count, RECV), 'length', split_axis=0, concat...  6.33 us
    unnamed x22, local copies, waits for them, and re-layouts  4.96 us
  transfers between devices with their start and end apart: 1, of which 0 were waited for; matrix products, arithmetic and copies ran while one was open for 0% of the time, Pallas kernels for 19%

profile of v1, /device:TPU:0, one launch (start us, length us, event | category | flops | bytes accessed | tf_op | source)
XLA Modules:
  0.0 41.8 jit_solution(14375771870937091187)
XLA Ops:
  0.6 0.0 copy-start.9
  0.6 0.0 copy-start.10
  0.7 0.0 copy-start
  0.7 1.4 %copy-done = bf16[1,1,32,25,1024]{4,2,3,1,0:T(8,128)(2,1)S(1)} copy-done((bf16[1,1,32,25,1024]{4,2,3,1,0:T(8,128)(2,1)S(1)}, bf16[1,1,32,25,1024]{4,2,3,1,0:T(8,128)(2,1)}, u32[]{:S(2)}) %copy-start) | copy-done | bytes 1638424
  2.1 0.0 copy-start.1
  2.1 1.0 %copy-done.1 = bf16[1,1,32,8,1024]{4,3,2,1,0:T(8,128)(2,1)S(1)} copy-done((bf16[1,1,32,8,1024]{4,3,2,1,0:T(8,128)(2,1)S(1)}, bf16[1,1,32,8,1024]{4,3,2,1,0:T(8,128)(2,1)}, u32[]{:S(2)}) %copy-start.1) | copy-done | bytes 524312
  3.1 0.0 copy-start.4
  3.1 0.9 %copy-done.4 = s32[1,1,32,1024]{3,2,1,0:T(8,128)S(1)} copy-done((s32[1,1,32,1024]{3,2,1,0:T(8,128)S(1)}, s32[1,1,32,1024]{3,2,1,0:T(8,128)}, u32[]{:S(2)}) %copy-start.4) | copy-done | bytes 131096
  4.0 0.0 copy-start.5
  4.0 0.9 %copy-done.5 = s32[1,1,32,1024]{3,2,1,0:T(8,128)S(1)} copy-done((s32[1,1,32,1024]{3,2,1,0:T(8,128)S(1)}, s32[1,1,32,1024]{3,2,1,0:T(8,128)}, u32[]{:S(2)}) %copy-start.5) | copy-done | bytes 131096
  4.9 0.0 copy-start.8
  5.0 0.7 %copy-done.8 = s32[1,1,32]{2,1,0:T(1,128)S(1)} copy-done((s32[1,1,32]{2,1,0:T(1,128)S(1)}, s32[1,1,32]{2,1,0:T(1,128)}, u32[]{:S(2)}) %copy-start.8) | copy-done | bytes 152
  5.6 0.0 copy-start.2
  5.6 0.0 copy-start.3
  5.6 0.0 copy-start.6
  5.6 0.0 copy-start.7
  5.6 20.6 %shard_map.121 = (bf16[1,1,25,32,1024]{4,3,2,1,0:T(8,128)(2,1)}, f32[8,128]{1,0:T(8,128)S(1)}) custom-call(s32[32]{0:T(128)S(1)} %bitcast.22, bf16[1,1,25,32,1024]{4,3,2,1,0:T(8,128)(2,1)S(1)} %bitcast.16, bf16[1,1,32,8,1024]{4,3,2,1,0:T(8,128)(2,1)S(1)} %copy-done.1, s32[32,1024]{1,0:T(8,128)S(1)} %bitcast.18, s32[32,1024]{1,0:T(8,128)S(1)} %bitcast.19), custom_call_target="tpu_custom_call" | custom-call | tf_op jit(solution)/shard_map/pallas_call | solution.py:287
  26.2 0.1 reduce_sum.35
  26.3 0.0 copy-done.9
  26.3 0.0 copy-done.10
  26.3 0.1 select_reduce_fusion
  26.4 0.7 %all_to_all.6 = f32[4,1,16]{2,0,1:T(4,128)} reshape(f32[64]{0:T(128)S(1)} %select_reduce_fusion) | data formatting | bytes 512 | tf_op jit(solution)/shard_map/all_to_all | solution.py:320
  27.1 6.3 %all-to-all-start = ((f32[4,1,16]{2,1,0:T(1,128)}), f32[4,1,16]{2,1,0:T(1,128)S(1)}, u32[]{:S(2)}, u32[]{:S(2)}) async-start(f32[4,1,16]{2,1,0:T(1,128)} %bitcast.10), calls=%async_computation | async-start | bytes 4096 | tf_op jit(solution)/shard_map/all_to_all | solution.py:320
  33.4 0.0 copy-done.2
  33.4 0.0 copy-done.3
  33.4 0.0 copy-done.6
  33.5 0.0 copy-done.7
  33.5 7.8 %shard_map.122 = (bf16[1,1,25,8,1024]{4,3,2,1,0:T(8,128)(2,1)}, f32[8,128]{1,0:T(8,128)}) custom-call(s32[8]{0:T(128)S(1)} %broadcast_1_dest_ref.2.dest_ref, bf16[1,1,25,8,1024]{4,3,2,1,0:T(8,128)(2,1)S(1)} %bitcast.17, bf16[1,1,8,8,1024]{4,3,2,1,0:T(8,128)(2,1)S(1)} %copy-done.3, s32[8,1024]{1,0:T(8,128)S(1)} %bitcast.20, s32[8,1024]{1,0:T(8,128)S(1)} %bitcast.21), custom_call_target="tpu_custom_call" | custom-call | tf_op jit(solution)/shard_map/pallas_call | solution.py:287
  41.3 0.0 all-to-all-done
  41.3 0.5 %reduce_sum.38 = f32[16]{0:T(128)} reduce(f32[4,1,16]{2,1,0:T(1,128)S(1)} %all-to-all-done, f32[]{:T(128)} %constant.3.clone.1), dimensions={0,1}, to_apply=%region_3.4 | reduce | flops 48 | bytes 324 | tf_op jit(solution)/shard_map/reduce_sum | solution.py:324
  (5 shorter events, 0.1 us)
Async XLA Ops:
  0.6 25.7 %copy-start.9 = (s32[1,1,32]{2,1,0:T(1,128)S(1)}, s32[1,1,32]{2,1,0:T(1,128)}, u32[]{:S(2)}) copy-start(s32[1,1,32]{2,1,0:T(1,128)} %param.14) | copy-start | bytes 388
  0.6 25.7 %copy-start.10 = (s32[1,1,32]{2,1,0:T(1,128)S(1)}, s32[1,1,32]{2,1,0:T(1,128)}, u32[]{:S(2)}) copy-start(s32[1,1,32]{2,1,0:T(1,128)} %param.15) | copy-start | bytes 388
  0.7 1.4 %copy-start = (bf16[1,1,32,25,1024]{4,2,3,1,0:T(8,128)(2,1)S(1)}, bf16[1,1,32,25,1024]{4,2,3,1,0:T(8,128)(2,1)}, u32[]{:S(2)}) copy-start(bf16[1,1,32,25,1024]{4,2,3,1,0:T(8,128)(2,1)} %param.10) | copy-start | bytes 4915204
  2.1 1.0 %copy-start.1 = (bf16[1,1,32,8,1024]{4,3,2,1,0:T(8,128)(2,1)S(1)}, bf16[1,1,32,8,1024]{4,3,2,1,0:T(8,128)(2,1)}, u32[]{:S(2)}) copy-start(bf16[1,1,32,8,1024]{4,3,2,1,0:T(8,128)(2,1)} %u_ref.2) | copy-start | bytes 1572868
  3.1 0.9 %copy-start.4 = (s32[1,1,32,1024]{3,2,1,0:T(8,128)S(1)}, s32[1,1,32,1024]{3,2,1,0:T(8,128)}, u32[]{:S(2)}) copy-start(s32[1,1,32,1024]{3,2,1,0:T(8,128)} %param.12) | copy-start | bytes 393220
  4.0 0.9 %copy-start.5 = (s32[1,1,32,1024]{3,2,1,0:T(8,128)S(1)}, s32[1,1,32,1024]{3,2,1,0:T(8,128)}, u32[]{:S(2)}) copy-start(s32[1,1,32,1024]{3,2,1,0:T(8,128)} %param.13) | copy-start | bytes 393220
  4.9 0.7 %copy-start.8 = (s32[1,1,32]{2,1,0:T(1,128)S(1)}, s32[1,1,32]{2,1,0:T(1,128)}, u32[]{:S(2)}) copy-start(s32[1,1,32]{2,1,0:T(1,128)} %param.14) | copy-start | bytes 388
  5.6 27.8 %copy-start.2 = (bf16[1,1,8,25,1024]{4,2,3,1,0:T(8,128)(2,1)S(1)}, bf16[1,1,8,25,1024]{4,2,3,1,0:T(8,128)(2,1)}, u32[]{:S(2)}) copy-start(bf16[1,1,8,25,1024]{4,2,3,1,0:T(8,128)(2,1)} %param.16) | copy-start | bytes 1228804
  5.6 27.8 %copy-start.3 = (bf16[1,1,8,8,1024]{4,3,2,1,0:T(8,128)(2,1)S(1)}, bf16[1,1,8,8,1024]{4,3,2,1,0:T(8,128)(2,1)}, u32[]{:S(2)}) copy-start(bf16[1,1,8,8,1024]{4,3,2,1,0:T(8,128)(2,1)} %u_ref.3) | copy-start | bytes 393220
  5.6 27.8 %copy-start.6 = (s32[1,1,8,1024]{3,2,1,0:T(8,128)S(1)}, s32[1,1,8,1024]{3,2,1,0:T(8,128)}, u32[]{:S(2)}) copy-start(s32[1,1,8,1024]{3,2,1,0:T(8,128)} %param.18) | copy-start | bytes 98308
  5.6 27.8 %copy-start.7 = (s32[1,1,8,1024]{3,2,1,0:T(8,128)S(1)}, s32[1,1,8,1024]{3,2,1,0:T(8,128)}, u32[]{:S(2)}) copy-start(s32[1,1,8,1024]{3,2,1,0:T(8,128)} %param.19) | copy-start | bytes 98308
  27.1 14.2 %all-to-all-start = ((f32[4,1,16]{2,1,0:T(1,128)}), f32[4,1,16]{2,1,0:T(1,128)S(1)}, u32[]{:S(2)}, u32[]{:S(2)}) async-start(f32[4,1,16]{2,1,0:T(1,128)} %bitcast.10), calls=%async_computation | async-start | bytes 4096 | tf_op jit(solution)/shard_map/all_to_all | solution.py:320

commit v2 on v1

v2 whole, which is shorter than its diff:
```python
import functools

import jax
import jax.numpy as jnp
from jax import lax
from jax.experimental import pallas as pl
from jax.experimental.pallas import tpu as pltpu
from jax.sharding import PartitionSpec as P

CLASSES = 8
FREE = CLASSES - 1
TAPS = 25
TILE = 32
ITERS = 3
RECV = 16
LANES = 128
COLS = 4
PAIR = 2


def total(values):
    while len(values) > 1:
        values = [sum(values[i : i + 2]) for i in range(0, len(values), 2)]
    return values[0]


def nt(x, y):
    return lax.dot_general(x, y, (((1,), (1,)), ((), ())), preferred_element_type=jnp.float32)


def turned(x, carry):
    return x if carry == 0 else pltpu.roll(x, 7 if carry > 0 else 1, 0)


def passed(x, carry, tiles):
    return x if carry == 0 else pltpu.roll(x, LANES - tiles if carry > 0 else tiles, 1)


def message(kern, field, q):
    acc = [[None] * COLS for _ in range(FREE)]
    for a in range(5):
        for p in range(COLS + 4):
            near = [field[c, q + a, p] for c in range(FREE)]
            for o in range(COLS):
                b = p - o
                if 0 <= b < 5:
                    k = kern[5 * a + b, q, o]
                    for c in range(FREE):
                        x = k * near[c]
                        acc[c][o] = x if acc[c][o] is None else acc[c][o] + x
    return acc


def put_row(field, c, row, values):
    for p in range(-2, COLS + 2):
        field[c, row, p + 2] = turned(values[p % COLS], p // COLS)


def put_edges(field, rows, tiles):
    for c in range(FREE):
        for e in range(2):
            for source, target, carry in ((e, rows + e, 1), (rows - 2 + e, e - 2, -1)):
                values = [passed(field[c, source + 2, p + 2], carry, tiles) for p in range(COLS)]
                put_row(field, c, target + 2, values)


def column(row):
    n = row.shape[1]
    own = lax.broadcasted_iota(jnp.int32, (n, n), 0) == lax.broadcasted_iota(jnp.int32, (n, n), 1)
    return jnp.sum(jnp.where(own, row, 0.0), axis=1, keepdims=True)


def tile_steps(after_loss, lists, k_ref, u_ref, lab_ref, mask_ref, grad_ref, loss_ref, dest_buf, scratch):
    kf, kb, raw, un, tgt, prob, fld, gfld, out, kbuf, ubuf, lab_buf, mask_buf, gbuf = scratch[:14]
    sems, out_sems = scratch[14:]
    lead = lists is not None
    tiles = lab_ref.shape[0]
    groups = LANES // tiles
    rows = TILE // groups
    depth = rows * TILE
    lane = lax.broadcasted_iota(jnp.int32, (8, LANES), 1)
    sub = lax.broadcasted_iota(jnp.int32, (8, LANES), 0)
    one = jnp.ones((8, LANES), jnp.float32)
    width = max(depth, LANES)
    halves = width // depth
    chunks = groups // halves
    low = lane // tiles % 2 == 0

    load_u = pltpu.make_async_copy(u_ref.at[0, 0], ubuf, sems.at[5])
    load_k = [
        pltpu.make_async_copy(
            k_ref.at[0, 0, pl.ds(5 * a, 5)], kbuf.at[pl.ds(5 * a, 5)], sems.at[a]
        )
        for a in range(5)
    ]
    load_lab = pltpu.make_async_copy(lab_ref, lab_buf, sems.at[6])
    load_mask = pltpu.make_async_copy(mask_ref, mask_buf, sems.at[7])
    for load in (load_u, *load_k, load_lab, load_mask):
        load.start()
    yield

    def spot(x):
        return x // TILE * TILE + x % 8 * COLS + x // 8 % COLS

    row = lax.broadcasted_iota(jnp.int32, (width, width), 0)
    col = lax.broadcasted_iota(jnp.int32, (width, width), 1)
    gather = jnp.where(col == row // depth * depth + spot(row % depth), 1.0, 0.0)
    gather = gather.astype(jnp.bfloat16)
    row = lax.broadcasted_iota(jnp.int32, (chunks * tiles, LANES), 0)
    col = lax.broadcasted_iota(jnp.int32, (chunks * tiles, LANES), 1)
    scatter = (row % tiles == col % tiles) & (row // tiles == col // (tiles * halves))
    scatter = jnp.where(scatter, 1.0, 0.0).astype(jnp.bfloat16)

    def to_fields(part):
        pieces = [part(g) for g in range(chunks) for _ in range(halves)]
        turn = nt(gather, jnp.concatenate(pieces, axis=0).astype(jnp.bfloat16))
        both = lambda n: turn[8 * n : 8 * n + 8]
        regs = [
            both(n) if halves == 1 else jnp.where(low, both(n), both(n + rows * COLS))
            for n in range(rows * COLS)
        ]
        return [regs[q * COLS : (q + 1) * COLS] for q in range(rows)]

    def inside(a, b, q, o):
        ok = None
        if not 0 <= o + b < COLS:
            ok = sub > 0 if o + b < 0 else sub < 7
        if not 0 <= q + a < rows:
            near = lane >= tiles if q + a < 0 else lane < LANES - tiles
            ok = near if ok is None else ok & near
        return ok

    load_u.wait()

    @pl.loop(0, tiles)
    def _(j):
        for p in range(8):
            raw[p, pl.ds(pl.multiple_of(j * CLASSES, CLASSES), CLASSES), :] = ubuf[
                j, :, LANES * p : LANES * (p + 1)
            ].astype(jnp.float32)

    def scores(c):
        def part(g):
            span = width // LANES
            rows_of = pl.ds(c, tiles, stride=CLASSES)
            return jnp.concatenate([raw[span * g + n, rows_of, :] for n in range(span)], axis=1)

        return to_fields(part)

    last = scores(FREE)
    for c in range(FREE):
        own = scores(c)
        for q in range(rows):
            for o in range(COLS):
                un[c, q, o] = own[q][o] - last[q][o]

    def soft(i, q, logits):
        values = [[None] * COLS for _ in range(FREE)]
        for o in range(COLS):
            raised = [jnp.exp(logits[c][o]) for c in range(FREE)]
            scale = 1.0 / total(raised + [one])
            for c in range(FREE):
                belief = raised[c] * scale
                prob[i, c, q, o] = belief
                values[c][o] = belief - scale
        for c in range(FREE):
            put_row(fld.at[i], c, q + 2, values[c])

    @pl.loop(0, rows)
    def _(q):
        soft(0, q, [[un[c, q, o] for o in range(COLS)] for c in range(FREE)])

    if lead:
        put_edges(fld.at[0], rows, tiles)
    yield

    for a in range(-2, 3):
        load_k[a + 2].wait()
        for b in range(-2, 3):
            t = 5 * (a + 2) + b + 2
            regs = to_fields(
                lambda g: kbuf[t, :, width * g : width * (g + 1)].astype(jnp.float32)
            )
            for q in range(rows):
                for o in range(COLS):
                    ok = inside(a, b, q, o)
                    if ok is not None:
                        regs[q][o] = jnp.where(ok, regs[q][o], 0.0)
                    kf[t, q, o] = regs[q][o]
            for q in range(rows):
                for o in range(COLS):
                    x = turned(regs[(q - a) % rows][(o - b) % COLS], (o - b) // COLS)
                    kb[TAPS - 1 - t, q, o] = passed(x, (q - a) // rows, tiles)

    load_lab.wait()
    load_mask.wait()
    if lead:
        for load in lists:
            load.wait()
        listed = column(dest_buf[...].astype(jnp.float32)) >= 0.0
        listed = jnp.broadcast_to(jnp.where(listed, 1, 0), (tiles, width))

    def targets(g):
        part = slice(width * g, width * (g + 1))
        used = mask_buf[:, part] == 1
        if lead:
            used = used & (listed == 1)
        return jnp.where(used, lab_buf[:, part], CLASSES).astype(jnp.float32)

    for q, regs in enumerate(to_fields(targets)):
        for o in range(COLS):
            tgt[q, o] = regs[o]

    yield

    def pairs(work):
        if rows > PAIR:
            pl.loop(0, rows // PAIR)(work)
        else:
            work(0)

    def sweep(i, q):
        sent = message(kf, fld.at[i], q)
        return [[un[c, q, o] + sent[c][o] for o in range(COLS)] for c in range(FREE)]

    def forward(i, m):
        for n in range(PAIR):
            q = PAIR * m + n
            soft(i + 1, q, sweep(i, q))

    def final(m):
        for n in range(PAIR):
            q = PAIR * m + n
            logits = sweep(ITERS - 1, q)
            values = [[None] * COLS for _ in range(FREE)]
            for o in range(COLS):
                raised = [jnp.exp(logits[c][o]) for c in range(FREE)]
                summed = total(raised + [one])
                labels = tgt[q, o]
                used = labels < CLASSES
                picked = [labels == c for c in range(FREE)]
                if loss_ref is not None:
                    chosen = total([jnp.where(picked[c], logits[c][o], 0.0) for c in range(FREE)])
                    loss_ref[...] += jnp.where(used, jnp.log(summed) - chosen, 0.0)
                scale = jnp.where(used, 1.0 / summed, 0.0)
                for c in range(FREE):
                    values[c][o] = raised[c] * scale - jnp.where(picked[c], 1.0, 0.0)
            for c in range(FREE):
                put_row(gfld.at[ITERS - 1], c, q + 2, values[c])

    def backward(i, m):
        for n in range(PAIR):
            q = PAIR * m + n
            back = message(kb, gfld.at[i], q)
            values = [[None] * COLS for _ in range(FREE)]
            for o in range(COLS):
                mean = total([back[c][o] * fld[i, c, q + 2, o + 2] for c in range(FREE)])
                for c in range(FREE):
                    values[c][o] = prob[i, c, q, o] * (back[c][o] - mean)
            for c in range(FREE):
                put_row(gfld.at[i - 1], c, q + 2, values[c])

    if loss_ref is not None:
        loss_ref[...] = jnp.zeros((8, LANES), jnp.float32)
    works = [
        (functools.partial(forward, 0), fld.at[0]),
        (functools.partial(forward, 1), fld.at[1]),
        (final, fld.at[2]),
        (functools.partial(backward, 2), gfld.at[2]),
        (functools.partial(backward, 1), gfld.at[1]),
    ]
    for n, (work, field) in enumerate(works):
        if not lead:
            put_edges(field, rows, tiles)
        pairs(work)
        if lead and n + 1 < len(works):
            put_edges(works[n + 1][1], rows, tiles)
        if lead and work is final:
            after_loss()
        yield

    def store(a):
        part = pl.ds(5 * a, 5)
        return pltpu.make_async_copy(gbuf.at[part], grad_ref.at[0, 0, part], out_sems.at[a])

    @pl.loop(0, 5)
    def _(a):
        @pl.loop(0, rows // PAIR)
        def _(m):
            def step(i, flat):
                flat = list(flat)
                for c in range(FREE):
                    for r in range(PAIR):
                        q = PAIR * m + r
                        slope = [gfld[i, c, q + 2, o + 2] for o in range(COLS)]
                        for p in range(COLS + 4):
                            x = fld[i, c, q + a, p]
                            for o in range(COLS):
                                b = p - o
                                if 0 <= b < 5:
                                    n = (r * 5 + b) * COLS + o
                                    flat[n] = flat[n] + slope[o] * x
                return flat

            zeros = [jnp.zeros((8, LANES), jnp.float32)] * (PAIR * 5 * COLS)
            flat = lax.fori_loop(0, ITERS, step, zeros)
            for r in range(PAIR):
                q = PAIR * m + r
                place = lane // tiles * rows + q + a - 2
                ok = (place >= 0) & (place < TILE)
                for b in range(5):
                    for o in range(COLS):
                        near = ok
                        if not 0 <= o + b - 2 < COLS:
                            near = near & (sub > 0 if o + b < 2 else sub < 7)
                        spots = pl.ds(q * TILE + o, 8, stride=COLS)
                        x = flat[(r * 5 + b) * COLS + o]
                        out[5 * a + b, spots, :] = jnp.where(near, x, 0.0)

    yield
    for t in range(TAPS):
        flat = out[t]
        if halves > 1:
            even = lax.broadcasted_iota(jnp.int32, flat.shape, 1) // tiles % 2 == 0
            flat = jnp.concatenate([jnp.where(even, flat, 0.0), jnp.where(even, 0.0, flat)], axis=0)
        back = nt(scatter, flat.astype(jnp.bfloat16)).astype(jnp.bfloat16)
        for g in range(chunks):
            gbuf[t, :, width * g : width * (g + 1)] = back[tiles * g : tiles * (g + 1)]
        if t % 5 == 4:
            store(t // 5).start()
    yield
    for a in range(5):
        store(a).wait()


def crf_kernel(*refs):
    dest_ref, slot_ref, flagged, resident = refs[0], refs[1], refs[2:6], refs[6:10]
    flag_grad, res_grad, table_ref = refs[10:13]
    loss_buf, dest_buf, slot_buf, table_buf, list_sems = refs[13:18]
    scratch = refs[18:]
    half = len(scratch) // 2
    lists = [
        pltpu.make_async_copy(dest_ref, dest_buf, list_sems.at[0]),
        pltpu.make_async_copy(slot_ref, slot_buf, list_sems.at[1]),
    ]
    for load in lists:
        load.start()
    leave = pltpu.make_async_copy(table_buf, table_ref, list_sems.at[2])

    def tabulate():
        amount = dest_buf.shape[1]
        row = jnp.sum(loss_buf[...], axis=0, keepdims=True)
        shift = amount
        while shift < LANES:
            row = row + pltpu.roll(row, shift, 1)
            shift *= 2
        losses = column(row[:, :amount]) / TILE
        dests = column(dest_buf[...].astype(jnp.float32))
        slots = column(slot_buf[...].astype(jnp.float32))
        place = lax.broadcasted_iota(jnp.int32, (amount, LANES), 1).astype(jnp.float32)
        for d in range(table_buf.shape[0]):
            picked = jnp.where((dests == d) & (slots == place), losses, 0.0)
            table_buf[d] = jnp.broadcast_to(jnp.sum(picked, axis=0, keepdims=True), (8, LANES))
        leave.start()

    runs = [
        tile_steps(tabulate, lists, *flagged, flag_grad, loss_buf, dest_buf, scratch[:half]),
        tile_steps(None, None, *resident, res_grad, None, None, scratch[half:]),
    ]
    while runs:
        runs = [run for run in runs if next(run, True) is None]
    leave.wait()


def exchange_kernel(count, table_ref, help_ref, heard, send_sems, recv_sems, own_sem):
    me = lax.axis_index("length")
    peers = [(me + k) % count for k in range(1, count)]
    barrier = pltpu.get_barrier_semaphore()
    for peer in peers:
        pl.semaphore_signal(
            barrier, inc=1, device_id={"length": peer}, device_id_type=pl.DeviceIdType.MESH
        )
    own = pltpu.make_async_copy(table_ref.at[me], heard.at[count - 1], own_sem)
    own.start()
    pl.semaphore_wait(barrier, count - 1)
    sends = [
        pltpu.make_async_remote_copy(
            src_ref=table_ref.at[peer],
            dst_ref=heard.at[k],
            send_sem=send_sems.at[k],
            recv_sem=recv_sems.at[k],
            device_id={"length": peer},
            device_id_type=pl.DeviceIdType.MESH,
        )
        for k, peer in enumerate(peers)
    ]
    for send in sends:
        send.start()
    own.wait()
    summed = heard[count - 1]
    for k, send in enumerate(sends):
        send.wait()
        summed = summed + heard[k]
    help_ref[...] = summed


def scratch_for(kernels):
    taps, amount, pixels = kernels.shape[2:]
    rows = TILE * amount // LANES
    regs = lambda *lead: pltpu.VMEM((*lead, 8, LANES), jnp.float32)
    return [
        regs(taps, rows, COLS),
        regs(taps, rows, COLS),
        pltpu.VMEM((8, amount * CLASSES, LANES), jnp.float32),
        regs(FREE, rows, COLS),
        regs(rows, COLS),
        regs(ITERS, FREE, rows, COLS),
        regs(ITERS, FREE, rows + 4, COLS + 4),
        regs(ITERS, FREE, rows + 4, COLS + 4),
        pltpu.VMEM((taps, rows * TILE, LANES), jnp.float32),
        pltpu.VMEM((taps, amount, pixels), jnp.bfloat16),
        pltpu.VMEM((amount, CLASSES, pixels), jnp.bfloat16),
        pltpu.VMEM((amount, pixels), jnp.int32),
        pltpu.VMEM((amount, pixels), jnp.int32),
        pltpu.VMEM((taps, amount, pixels), jnp.bfloat16),
        pltpu.SemaphoreType.DMA((8,)),
        pltpu.SemaphoreType.DMA((5,)),
    ]


def on_device(fk, fu, fl, fm, dest, slot, rk, ru, rl, rm):
    count = lax.axis_size("length")
    fk, rk = jnp.swapaxes(fk, 2, 3), jnp.swapaxes(rk, 2, 3)
    hbm = pl.BlockSpec(memory_space=pltpu.HBM)
    vmem = pl.BlockSpec(memory_space=pltpu.VMEM)
    tile_field = jax.ShapeDtypeStruct((8, LANES), jnp.float32)
    listed = dest.shape[2]
    field = (8, LANES)
    flag_grad, res_grad, table = pl.pallas_call(
        crf_kernel,
        in_specs=[hbm] * 10,
        out_specs=[hbm] * 3,
        scratch_shapes=[
            pltpu.VMEM(field, jnp.float32),
            pltpu.VMEM((1, listed), jnp.int32),
            pltpu.VMEM((1, listed), jnp.int32),
            pltpu.VMEM((count, *field), jnp.float32),
            pltpu.SemaphoreType.DMA((3,)),
            *scratch_for(fk),
            *scratch_for(rk),
        ],
        out_shape=[
            jax.ShapeDtypeStruct(fk.shape, jnp.bfloat16),
            jax.ShapeDtypeStruct(rk.shape, jnp.bfloat16),
            jax.ShapeDtypeStruct((count, *field), jnp.float32),
        ],
        compiler_params=pltpu.CompilerParams(vmem_limit_bytes=63_400_000),
    )(dest[0], slot[0], fk, fu, fl[0, 0], fm[0, 0], rk, ru, rl[0, 0], rm[0, 0])
    helped = pl.pallas_call(
        functools.partial(exchange_kernel, count),
        in_specs=[hbm],
        out_specs=vmem,
        scratch_shapes=[
            pltpu.VMEM((count, *field), jnp.float32),
            pltpu.SemaphoreType.DMA((count - 1,)),
            pltpu.SemaphoreType.DMA((count - 1,)),
            pltpu.SemaphoreType.DMA,
        ],
        out_shape=jax.ShapeDtypeStruct(field, jnp.float32),
        compiler_params=pltpu.CompilerParams(
            collective_id=0, has_side_effects=True, vmem_limit_bytes=4 * 1024 * 1024
        ),
    )(table)
    return jnp.swapaxes(flag_grad, 2, 3), jnp.swapaxes(res_grad, 2, 3), helped[None, :1, :RECV]


def solution(mesh):
    tile_axes = ("groups", "sector", "pair")
    spec = lambda n: P("length", tile_axes, *([None] * n))
    return jax.shard_map(
        on_device,
        mesh=mesh,
        in_specs=(spec(3), spec(3), spec(2), spec(2), spec(1), spec(1), spec(3), spec(3), spec(2), spec(2)),
        out_specs=(spec(3), spec(3), spec(1)),
        check_vma=False,
    )
```

time: 42.1 us -> 38.1 us (0.905)
  Pallas kernels: 28.4 us -> 36 us
  starting transfers between devices: 6.33 us -> 0 us
  local copies, waits for them, and re-layouts: 5.71 us -> 1.22 us
  other arithmetic: 0.68 us -> 0 us
    pallas_call x2, Pallas kernels: 28.4 us -> 36 us  [the longest x1 28.7 us: on_device(): pl.pallas_call(crf_kernel, in_specs=[hbm] * 10, out_specs=[hbm] * 3, scra...]
    all_to_all x1 -> x0, starting transfers between devices: 6.33 us -> none  [on_device(): lax.all_to_all(table.reshape(count, RECV), 'length', split_axis=0, concat...]
    unnamed x22 -> x2, local copies, waits for them, and re-layouts: 4.96 us -> 0.71 us
    reduce_sum x4 -> x0, other arithmetic: 0.66 us -> none  [the longest x1 0.53 us: on_device(): return (flag_grad, res_grad, jnp.sum(got, axis=0)[None, None])]
    all_to_all x1 -> x0, local copies, waits for them, and re-layouts: 0.66 us -> none  [on_device(): lax.all_to_all(table.reshape(count, RECV), 'length', split_axis=0, concat...]
    broadcast_in_dim x0 -> x1, local copies, waits for them, and re-layouts: none -> 0.51 us  [on_device(): helped[None, :1, :RECV]]
  transfers between devices with their start and end apart: 1 -> 0, of which waited for: 0 -> 0; matrix products, arithmetic and copies ran while one was open for 0% -> 0% of each run, Pallas kernels for 19% -> 0%
where the time goes in v2:
time: 38.1 us; the launch traced here: 37.8 us
  Pallas kernels  36 us (94%)
  local copies, waits for them, and re-layouts  1.22 us (3%)
  between operations  0.66 us (2%)
    pallas_call x1, Pallas kernels, on_device(): pl.pallas_call(crf_kernel, in_specs=[hbm] * 10, out_specs=[hbm] * 3, scra...  28.7 us
    pallas_call x1, Pallas kernels, on_device(): pl.pallas_call(functools.partial(exchange_kernel, count), in_specs=[hbm],...  7.3 us

profile of v2, /device:TPU:0, one launch (start us, length us, event | category | flops | bytes accessed | tf_op | source)
XLA Modules:
  0.0 37.8 jit_solution(10172984581281114758)
XLA Ops:
  0.6 28.7 %shard_map.121 = (bf16[1,1,25,32,1024]{4,3,2,1,0:T(8,128)(2,1)}, bf16[1,1,25,8,1024]{4,3,2,1,0:T(8,128)(2,1)}, f32[4,8,128]{2,1,0:T(8,128)}) custom-call(s32[1,32]{1,0:T(1,128)} %bitcast.18, s32[1,32]{1,0:T(1,128)} %bitcast.19, bf16[1,1,25,32,1024]{4,3,2,1,0:T(8,128)(2,1)} %bitcast.12, bf16[1,1,32,8,1024]{4,3,2,1,0:T(8,128)(2,1)} %refs_3_.1, ...), custom_call_target="tpu_custom_call" | custom-call | tf_op jit(solution)/shard_map/pallas_call | solution.py:439
  29.3 0.0 copy-start
  29.3 0.7 %copy-done = f32[4,8,128]{2,1,0:T(8,128)S(1)} copy-done((f32[4,8,128]{2,1,0:T(8,128)S(1)}, f32[4,8,128]{2,1,0:T(8,128)}, u32[]{:S(2)}) %copy-start) | copy-done | bytes 16408
  30.0 7.3 %shard_map.122 = f32[8,128]{1,0:T(8,128)S(1)} custom-call(f32[4,8,128]{2,1,0:T(8,128)S(1)} %copy-done), custom_call_target="tpu_custom_call" | custom-call | tf_op jit(solution)/shard_map/pallas_call | solution.py:459
  37.3 0.5 %slice_bitcast_fusion = f32[1,1,16]{2,1,0:T(1,128)} fusion(f32[8,128]{1,0:T(8,128)S(1)} %shard_map.122), kind=kLoop, calls=%fused_computation | loop fusion | bytes 128 | tf_op jit(solution)/shard_map/broadcast_in_dim | solution.py:474
Async XLA Ops:
  29.3 0.7 %copy-start = (f32[4,8,128]{2,1,0:T(8,128)S(1)}, f32[4,8,128]{2,1,0:T(8,128)}, u32[]{:S(2)}) copy-start(f32[4,8,128]{2,1,0:T(8,128)} %get-tuple-element.8.table_ref) | copy-start | bytes 49156

commit v3 on v2

--- a/solution.py
+++ b/solution.py
@@ -333,12 +333,11 @@
         store(a).wait()
 
 
-def crf_kernel(*refs):
-    dest_ref, slot_ref, flagged, resident = refs[0], refs[1], refs[2:6], refs[6:10]
-    flag_grad, res_grad, table_ref = refs[10:13]
-    loss_buf, dest_buf, slot_buf, table_buf, list_sems = refs[13:18]
-    scratch = refs[18:]
-    half = len(scratch) // 2
+def flagged_kernel(*refs):
+    dest_ref, slot_ref, flagged = refs[0], refs[1], refs[2:6]
+    flag_grad, table_ref = refs[6:8]
+    loss_buf, dest_buf, slot_buf, table_buf, list_sems = refs[8:13]
+    scratch = refs[13:]
     lists = [
         pltpu.make_async_copy(dest_ref, dest_buf, list_sems.at[0]),
         pltpu.make_async_copy(slot_ref, slot_buf, list_sems.at[1]),
@@ -363,16 +362,15 @@
             table_buf[d] = jnp.broadcast_to(jnp.sum(picked, axis=0, keepdims=True), (8, LANES))
         leave.start()
 
-    runs = [
-        tile_steps(tabulate, lists, *flagged, flag_grad, loss_buf, dest_buf, scratch[:half]),
-        tile_steps(None, None, *resident, res_grad, None, None, scratch[half:]),
-    ]
-    while runs:
-        runs = [run for run in runs if next(run, True) is None]
+    steps = tile_steps(tabulate, lists, *flagged, flag_grad, loss_buf, dest_buf, scratch)
+    for _ in steps:
+        pass
     leave.wait()
 
 
-def exchange_kernel(count, table_ref, help_ref, heard, send_sems, recv_sems, own_sem):
+def resident_kernel(count, table_ref, *refs):
+    resident, res_grad, help_ref = refs[:4], refs[4], refs[5]
+    heard, send_sems, recv_sems, own_sem = refs[6:10]
     me = lax.axis_index("length")
     peers = [(me + k) % count for k in range(1, count)]
     barrier = pltpu.get_barrier_semaphore()
@@ -381,8 +379,6 @@
             barrier, inc=1, device_id={"length": peer}, device_id_type=pl.DeviceIdType.MESH
         )
     own = pltpu.make_async_copy(table_ref.at[me], heard.at[count - 1], own_sem)
-    own.start()
-    pl.semaphore_wait(barrier, count - 1)
     sends = [
         pltpu.make_async_remote_copy(
             src_ref=table_ref.at[peer],
@@ -394,14 +390,19 @@
         )
         for k, peer in enumerate(peers)
     ]
-    for send in sends:
-        send.start()
+    steps = tile_steps(None, None, *resident, res_grad, None, None, refs[10:])
+    for n, _ in enumerate(steps):
+        if n == 3:
+            own.start()
+            pl.semaphore_wait(barrier, count - 1)
+            for send in sends:
+                send.start()
     own.wait()
     summed = heard[count - 1]
     for k, send in enumerate(sends):
         send.wait()
         summed = summed + heard[k]
-    help_ref[...] = summed
+    help_ref[...] = summed[0:1, :RECV]
 
 
 def scratch_for(kernels):
@@ -436,10 +437,10 @@
     tile_field = jax.ShapeDtypeStruct((8, LANES), jnp.float32)
     listed = dest.shape[2]
     field = (8, LANES)
-    flag_grad, res_grad, table = pl.pallas_call(
-        crf_kernel,
-        in_specs=[hbm] * 10,
-        out_specs=[hbm] * 3,
+    flag_grad, table = pl.pallas_call(
+        flagged_kernel,
+        in_specs=[hbm] * 6,
+        out_specs=[hbm] * 2,
         scratch_shapes=[
             pltpu.VMEM(field, jnp.float32),
             pltpu.VMEM((1, listed), jnp.int32),
@@ -447,31 +448,33 @@
             pltpu.VMEM((count, *field), jnp.float32),
             pltpu.SemaphoreType.DMA((3,)),
             *scratch_for(fk),
-            *scratch_for(rk),
         ],
         out_shape=[
             jax.ShapeDtypeStruct(fk.shape, jnp.bfloat16),
-            jax.ShapeDtypeStruct(rk.shape, jnp.bfloat16),
             jax.ShapeDtypeStruct((count, *field), jnp.float32),
         ],
         compiler_params=pltpu.CompilerParams(vmem_limit_bytes=63_400_000),
-    )(dest[0], slot[0], fk, fu, fl[0, 0], fm[0, 0], rk, ru, rl[0, 0], rm[0, 0])
-    helped = pl.pallas_call(
-        functools.partial(exchange_kernel, count),
-        in_specs=[hbm],
-        out_specs=vmem,
+    )(dest[0], slot[0], fk, fu, fl[0, 0], fm[0, 0])
+    res_grad, helped = pl.pallas_call(
+        functools.partial(resident_kernel, count),
+        in_specs=[hbm] * 5,
+        out_specs=[hbm, vmem],
         scratch_shapes=[
             pltpu.VMEM((count, *field), jnp.float32),
             pltpu.SemaphoreType.DMA((count - 1,)),
             pltpu.SemaphoreType.DMA((count - 1,)),
             pltpu.SemaphoreType.DMA,
+            *scratch_for(rk),
         ],
-        out_shape=jax.ShapeDtypeStruct(field, jnp.float32),
+        out_shape=[
+            jax.ShapeDtypeStruct(rk.shape, jnp.bfloat16),
+            jax.ShapeDtypeStruct((1, RECV), jnp.float32),
+        ],
         compiler_params=pltpu.CompilerParams(
-            collective_id=0, has_side_effects=True, vmem_limit_bytes=4 * 1024 * 1024
+            collective_id=0, has_side_effects=True, vmem_limit_bytes=63_400_000
         ),
-    )(table)
-    return jnp.swapaxes(flag_grad, 2, 3), jnp.swapaxes(res_grad, 2, 3), helped[None, :1, :RECV]
+    )(table, rk, ru, rl[0, 0], rm[0, 0])
+    return jnp.swapaxes(flag_grad, 2, 3), jnp.swapaxes(res_grad, 2, 3), helped[None]
 
 
 def solution(mesh):

time: 38.1 us -> 36.8 us (0.966)
  Pallas kernels: 36 us -> 33 us
  local copies, waits for them, and re-layouts: 1.22 us -> 2.9 us
    pallas_call x2, Pallas kernels: 36 us -> 33 us  [the longest x1 21.9 us: on_device(): pl.pallas_call(flagged_kernel, in_specs=[hbm] * 6, out_specs=[hbm] * 2, s...]
    unnamed x2, local copies, waits for them, and re-layouts: 0.71 us -> 2.9 us
    broadcast_in_dim x1 -> x0, local copies, waits for them, and re-layouts: 0.51 us -> none  [on_device(): helped[None, :1, :RECV]]
where the time goes in v3:
time: 36.8 us; the launch traced here: 36.5 us
  Pallas kernels  33 us (90%)
  local copies, waits for them, and re-layouts  2.9 us (8%)
  between operations  0.65 us (2%)
    pallas_call x1, Pallas kernels, on_device(): pl.pallas_call(flagged_kernel, in_specs=[hbm] * 6, out_specs=[hbm] * 2, s...  21.9 us
    pallas_call x1, Pallas kernels, on_device(): pl.pallas_call(functools.partial(resident_kernel, count), in_specs=[hbm]...  11.1 us
    unnamed x2, local copies, waits for them, and re-layouts  2.9 us

profile of v3, /device:TPU:0, one launch (start us, length us, event | category | flops | bytes accessed | tf_op | source)
XLA Modules:
  0.0 36.5 jit_solution(10144116917182750170)
XLA Ops:
  0.6 21.9 %shard_map.121 = (bf16[1,1,25,32,1024]{4,3,2,1,0:T(8,128)(2,1)}, f32[4,8,128]{2,1,0:T(8,128)}) custom-call(s32[1,32]{1,0:T(1,128)} %bitcast.18, s32[1,32]{1,0:T(1,128)} %bitcast.19, bf16[1,1,25,32,1024]{4,3,2,1,0:T(8,128)(2,1)} %bitcast.11, bf16[1,1,32,8,1024]{4,3,2,1,0:T(8,128)(2,1)} %refs_3_.1, s32[32,1024]{1,0:T(8,128)} %bitcast.14, s32[32,1024]{1,0:T(8,128)} %bitcast.15), custom_call_target="tpu_custom_call" | custom-call | tf_op jit(solution)/shard_map/pallas_call | solution.py:440
  22.5 11.1 %shard_map.122 = (bf16[1,1,25,8,1024]{4,3,2,1,0:T(8,128)(2,1)}, f32[1,16]{1,0:T(1,128)}) custom-call(f32[4,8,128]{2,1,0:T(8,128)} %get-tuple-element.8.table_ref, bf16[1,1,25,8,1024]{4,3,2,1,0:T(8,128)(2,1)} %bitcast.12, bf16[1,1,8,8,1024]{4,3,2,1,0:T(8,128)(2,1)} %refs_1_.1, s32[8,1024]{1,0:T(8,128)} %bitcast.16, s32[8,1024]{1,0:T(8,128)} %bitcast.17), custom_call_target="tpu_custom_call" | custom-call | tf_op jit(solution)/shard_map/pallas_call | solution.py:458
  33.6 1.8 %copy.15 = bf16[1,1,8,25,1024]{4,2,3,1,0:T(8,128)(2,1)} copy(bf16[1,1,8,25,1024]{4,2,3,1,0:T(8,128)(2,1)} %bitcast.13) | data formatting | bytes 819200
  35.4 1.1 %copy.16 = f32[1,1,16]{2,1,0:T(1,128)} copy(f32[1,1,16]{2,1,0:T(1,128)} %bitcast.21) | data formatting | bytes 128
